TPU v7x, 32 devices: a whole 2x2x4 slice. The times are simulated.
32 devices in a mesh: seq: 8 (over z, core), blk: 4 (over y, x).
Axes of the slice: x: 2, y: 2, z: 4, core: 2. Of those that a mesh axis runs over, the one named last changes fastest.
Arguments:
- tokens: bfloat16 [4096, 3072], P(('seq', 'blk')), may hold values from -8.6 to 8.6
- project_weight: bfloat16 [3, 3072, 2048], P(None, None, 'seq')
- noisy_latent: float32 [4096, 64], P(('seq', 'blk')), may hold values from -6 to 6
- final_weight: bfloat16 [2048, 64], replicated, may hold values from -0.5 to 0.5
- conv_weight: bfloat16 [432, 512], replicated, may hold values from -0.3125 to 0.3125
- norm_gain: float32 [512], replicated, may hold values from 0.1 to 1.9
- norm_shift: float32 [512], replicated, may hold values from -3 to 3
- owner_count: int32 [32], replicated, may hold values from 1 to 4, 64 in all
- intersection: int32 [64, 4], replicated, may hold values from 0 to 31, as said below
Outputs:
- decoded: bfloat16 [32, 4, 512, 2048], P(('seq', 'blk'))
Inputs may be any that keep to these rules, and one draw needn't show every extreme that they name: Owner o holds pixel tiles s to s + owner_count[o] - 1, s the sum of the counts below o; the counts sum to 64 and one owner holds exactly 4. `intersection`: row p names the four latent tiles of a 2 x 2 block of neighbouring tiles on a grid of 8 rows by 4 columns, tile r * 4 + c at row r, column c, in the order top left, top right, bottom left, bottom right.
All inputs are finite; a program needn't handle non-finite values.
Results may differ from a plain program's by a relative error of at most 0.014.
Values may be sent and summed in bfloat16 or wider, within the bound.
A program may use at most 128 MiB of HBM per device.

v0:
```python
import functools
import math

import jax
import jax.numpy as jnp
from jax import lax
from jax.experimental import pallas as pl
from jax.experimental.pallas import tpu as pltpu
from jax.sharding import PartitionSpec as P

HEAD_DIM = 128
LATENT_CH = 16
GROUPS = 32
TILE_F = 2
TILE_PH = 8
TILE_PW = 8
MAXPIX = 4

scale_factor = 0.476986
step_size = 0.25
norm_eps = 1e-06

REGION_ROWS = 4 * TILE_PH
REGION_COLS = 4 * TILE_PW
FRAME = REGION_ROWS * REGION_COLS
TAPS = 9 * LATENT_CH
MESH = pl.DeviceIdType.MESH
F32 = jnp.float32
BF16 = jnp.bfloat16
TILE_VOX = TILE_F * 4 * TILE_PH * TILE_PW


def nt_dot(a, b):
    return lax.dot_general(a, b, (((1,), (1,)), ((), ())), preferred_element_type=F32)


def attention_kernel(
    chain,
    n_blk,
    tokens_ref,
    weight_ref,
    noisy_ref,
    final_ref,
    conv_ref,
    gain_ref,
    shift_ref,
    tiles_ref,
    first_ref,
    second_ref,
    affine_ref,
    place_ref,
    tok,
    weight,
    q_all,
    kv_all,
    acc_all,
    max_all,
    vel_out,
    vel_in,
    own_tile,
    spread,
    first,
    second,
    affine,
    place,
    local_sem,
    keep_sem,
    tok_send,
    tok_recv,
    kv_send,
    kv_recv,
    vel_send,
    vel_recv,
    tile_send,
    tile_recv,
    over_send,
    over_recv,
):
    n_seq = 2 * chain
    seq = lax.axis_index("seq")
    blk = lax.axis_index("blk")
    z = lax.div(seq, 2)
    core = lax.rem(seq, 2)
    me = seq * n_blk + blk
    rows = tokens_ref.shape[0]
    half = rows // 2
    width = q_all.shape[2]
    heads = width // HEAD_DIM

    load_weight = pltpu.make_async_copy(weight_ref, weight, local_sem.at[0])
    load_weight.start()
    load_tokens = []
    for part in range(2):
        load_tokens.append(
            pltpu.make_async_copy(
                tokens_ref.at[pl.ds(part * half, half)],
                tok.at[z, part, core],
                local_sem.at[1 + part],
            )
        )
        load_tokens[part].start()

    barrier = pltpu.get_barrier_semaphore()

    def greet(step, carry):
        other = lax.rem(me + step, n_seq * n_blk)
        pl.semaphore_signal(
            barrier,
            inc=1,
            device_id=(lax.div(other, n_blk), lax.rem(other, n_blk)),
            device_id_type=MESH,
        )
        return carry

    lax.fori_loop(1, n_seq * n_blk, greet, 0)
    pl.semaphore_wait(barrier, n_seq * n_blk - 1)

    def tok_copy(origin, part, side, target_z, target_core):
        if origin is None:
            origin, source = z, tokens_ref.at[pl.ds(part * half, half)]
        else:
            source = tok.at[origin, part, core]
        return pltpu.make_async_remote_copy(
            src_ref=source,
            dst_ref=tok.at[origin, part, core],
            send_sem=tok_send.at[origin, part, side],
            recv_sem=tok_recv.at[origin, part, core],
            device_id=(target_z * 2 + target_core, blk),
            device_id_type=MESH,
        )

    def tok_arrival(origin, part, origin_core):
        pltpu.make_async_remote_copy(
            src_ref=tok.at[origin, part, origin_core],
            dst_ref=tok.at[origin, part, origin_core],
            send_sem=tok_send.at[origin, part, 0],
            recv_sem=tok_recv.at[origin, part, origin_core],
            device_id=(z * 2 + 1 - core, blk),
            device_id_type=MESH,
        ).wait_recv()

    def go_left(origin, part):
        return tok_copy(origin, part, 0, z - 1, core)

    def go_right(origin, part):
        return tok_copy(origin, part, 1, z + 1, core)

    def go_over(origin, part):
        return tok_copy(origin, part, 2, z, 1 - core)

    def kv_place(origin, part, source):
        return kv_all.at[origin, part, :, pl.ds(pl.multiple_of(source * rows, rows), rows), :]

    def kv_copy(origin, part, hop):
        return pltpu.make_async_remote_copy(
            src_ref=kv_place(origin, part, blk),
            dst_ref=kv_place(origin, part, blk),
            send_sem=kv_send.at[origin, part, hop],
            recv_sem=kv_recv.at[origin, part, blk],
            device_id=(seq, lax.rem(blk + hop, n_blk)),
            device_id_type=MESH,
        )

    def kv_arrival(origin, part, hop):
        source = lax.rem(blk + n_blk - hop, n_blk)
        pltpu.make_async_remote_copy(
            src_ref=kv_place(origin, part, source),
            dst_ref=kv_place(origin, part, source),
            send_sem=kv_send.at[origin, part, hop],
            recv_sem=kv_recv.at[origin, part, source],
            device_id=(seq, lax.rem(blk + hop, n_blk)),
            device_id_type=MESH,
        ).wait_recv()

    def project(origin, part):
        x = tok[origin, part].reshape(rows, tok.shape[4])
        own = pl.ds(pl.multiple_of(blk * rows, rows), rows)
        for kind in range(2):
            kv_all[origin, part, kind, own, :] = jnp.dot(
                x, weight[kind + 1], preferred_element_type=F32
            ).astype(BF16)
        for hop in range(1, n_blk):
            kv_copy(origin, part, hop).start()
        query = jnp.dot(x, weight[0], preferred_element_type=F32)
        query = (query * (HEAD_DIM**-0.5 * math.log2(math.e))).astype(BF16)
        some = pl.ds(part * rows, rows)
        q_all[origin, some, :] = query
        for head in range(heads):
            max_all[origin, head, some, :] = jnp.full((rows, HEAD_DIM), -1e30, F32)
            acc_all[origin, head, some, :] = jnp.zeros((rows, 2 * HEAD_DIM), F32)

    def attend(q_pair, kv_pair, part):
        for head in range(heads):
            lanes = pl.ds(head * HEAD_DIM, HEAD_DIM)
            scores = nt_dot(q_all[q_pair, :, lanes], kv_all[kv_pair, part, 0, :, lanes])
            old_max = max_all[q_pair, head]
            new_max = jnp.maximum(old_max, jnp.max(scores, axis=1, keepdims=True))
            rescale = jnp.exp2(old_max - new_max)
            weights = jnp.exp2(scores - new_max[:, :1]).astype(BF16)
            value = kv_all[kv_pair, part, 1, :, lanes]
            value = jnp.concatenate([value, jnp.ones_like(value)], axis=1)
            product = jnp.dot(weights, value, preferred_element_type=F32)
            acc_all[q_pair, head] = (
                acc_all[q_pair, head] * jnp.concatenate([rescale, rescale], axis=1) + product
            )
            max_all[q_pair, head] = new_max

    def each_of_step(step, action):
        if step >= chain:
            return
        if step == 0:
            action(z, None)
            return
        pl.when(z - step >= 0)(lambda: action(z - step, "left"))
        pl.when(z + step < chain)(lambda: action(z + step, "right"))

    def over_known(radius, action):
        low = jnp.maximum(z - radius, 0)
        high = jnp.minimum(z + radius, chain - 1) + 1

        def one(index, carry):
            action(index)
            return carry

        lax.fori_loop(low, high, one, 0)

    def forward(part):
        def action(origin, side):
            tok_arrival(origin, part, core)
            if side == "left":
                pl.when(z < chain - 1)(lambda: go_right(origin, part).start())
            else:
                pl.when(z > 0)(lambda: go_left(origin, part).start())
            go_over(origin, part).start()

        return action

    def project_arrived(part):
        def action(origin, side):
            tok_arrival(origin, part, 1 - core)
            project(origin, part)

        return action

    for part in range(2):
        pl.when(z > 0)(lambda: go_left(None, part).start())
        pl.when(z < chain - 1)(lambda: go_right(None, part).start())
        go_over(None, part).start()

    def prepare():
        token = lax.broadcasted_iota(jnp.int32, (rows, TILE_VOX), 0)
        voxel = lax.broadcasted_iota(jnp.int32, (rows, TILE_VOX), 1)
        row, column = (voxel >> 4) & 15, voxel & 15
        home = (voxel >> 8) * (TILE_PH * TILE_PW) + (row >> 1) * TILE_PW + (column >> 1)
        for sub in range(4):
            hit = (home == token) & ((row & 1) * 2 + (column & 1) == sub)
            spread[sub] = jnp.where(hit, 1.0, 0.0).astype(BF16)
        taps = [conv_ref[pl.ds(a * TAPS, TAPS), :].astype(F32) for a in range(3)]
        early = taps[0] + taps[1]
        first[...] = (early + taps[2]).T.astype(BF16)
        second[...] = jnp.concatenate([early, taps[2]], axis=0).T.astype(BF16)
        channels = conv_ref.shape[1]
        index = lax.broadcasted_iota(jnp.int32, (128, channels), 0)
        affine[...] = jnp.where(index == 0, gain_ref[...], shift_ref[...]).T
        source = lax.broadcasted_iota(jnp.int32, place.shape, 0)
        target = lax.broadcasted_iota(jnp.int32, place.shape, 1)
        wanted = ((source >> 4) & 15) * REGION_COLS + (source >> 8) * 16 + (source & 15)
        place[...] = jnp.where(wanted == target, 1.0, 0.0).astype(BF16)
        for copy in keeps:
            copy.start()

    keeps = [
        pltpu.make_async_copy(source, target, keep_sem.at[number])
        for number, (source, target) in enumerate(
            [(first, first_ref), (second, second_ref), (affine, affine_ref), (place, place_ref)]
        )
    ]

    load_weight.wait()
    load_tokens[0].wait()
    load_tokens[1].wait()
    for part in range(2):
        project_arrived(part)(z, None)

    def attend_both(q_pair, kv_pair):
        attend(q_pair, kv_pair, 0)
        attend(q_pair, kv_pair, 1)

    for turn in range(2 * chain):
        step, part = turn // 2, turn % 2
        if turn >= 1:
            each_of_step((turn + 1) // 2, forward((turn + 1) % 2))
            each_of_step((turn + 1) // 2, project_arrived((turn + 1) % 2))
        if turn == 0:
            prepare()
        if part == 0 and step >= 1:
            each_of_step(
                step, lambda o, side: over_known(step - 1, lambda other: attend_both(o, other))
            )

        def meet(origin, side):
            for hop in range(1, n_blk):
                kv_arrival(origin, part, hop)
            over_known(step, lambda other: attend(other, origin, part))

        each_of_step(step, meet)

    final = final_ref[:, pl.ds(pl.multiple_of(seq * width, width), width)]

    def vel_copy(target_z, target_core):
        target = target_z * 2 + target_core
        return pltpu.make_async_remote_copy(
            src_ref=vel_out.at[target],
            dst_ref=vel_in.at[seq],
            send_sem=vel_send.at[target],
            recv_sem=vel_recv.at[seq],
            device_id=(target, blk),
            device_id_type=MESH,
        )

    for turn in range(chain):
        q_pair = lax.rem(z + 1 + turn, chain)
        attended = []
        for head in range(heads):
            total = acc_all[q_pair, head]
            attended.append((total[:, :HEAD_DIM] / total[:, HEAD_DIM:]).astype(BF16))
        attended = jnp.concatenate(attended, axis=1)
        for side in range(2):
            own = [
                attended[part * rows + side * half : part * rows + (side + 1) * half]
                for part in range(2)
            ]
            vel_out[q_pair * 2 + side] = nt_dot(final, jnp.concatenate(own, axis=0)).astype(BF16)
        if turn < chain - 1:
            for side in range(2):
                vel_copy(q_pair, side).start()
        else:
            vel_copy(z, 1 - core).start()
    vel_in[seq] = vel_out[seq]

    def vel_arrival(hop, carry):
        source = lax.rem(seq + hop, n_seq)
        pltpu.make_async_remote_copy(
            src_ref=vel_out.at[source],
            dst_ref=vel_in.at[source],
            send_sem=vel_send.at[source],
            recv_sem=vel_recv.at[source],
            device_id=(source, blk),
            device_id_type=MESH,
        ).wait_recv()
        return carry

    lax.fori_loop(1, n_seq, vel_arrival, 0)
    velocity = vel_in[0].astype(F32)
    for source in range(1, n_seq):
        velocity = velocity + vel_in[source].astype(F32)
    patch = noisy_ref.shape[0]
    latent = ((noisy_ref[...] - step_size * velocity) / scale_factor).astype(BF16)
    channel = lax.broadcasted_iota(jnp.int32, (LATENT_CH, patch), 0)
    feature = lax.broadcasted_iota(jnp.int32, (LATENT_CH, patch), 1)
    tile = jnp.zeros((LATENT_CH, TILE_VOX), F32)
    for sub in range(4):
        pick = jnp.where(feature == channel * 4 + sub, 1.0, 0.0).astype(BF16)
        tile = tile + jnp.dot(
            jnp.dot(pick, latent, preferred_element_type=F32).astype(BF16),
            spread[sub],
            preferred_element_type=F32,
        )
    own_tile[...] = tile.astype(BF16)

    n_same = chain * n_blk
    index = z * n_blk + blk
    keep = pltpu.make_async_copy(own_tile, tiles_ref.at[z, core, blk], local_sem.at[0])
    keep.start()

    def tile_copy(hop):
        other = lax.rem(index + hop, n_same)
        return pltpu.make_async_remote_copy(
            src_ref=own_tile,
            dst_ref=tiles_ref.at[z, core, blk],
            send_sem=tile_send.at[hop],
            recv_sem=tile_recv.at[index],
            device_id=(lax.div(other, n_blk) * 2 + core, lax.rem(other, n_blk)),
            device_id_type=MESH,
        )

    def tile_start(hop, carry):
        tile_copy(hop).start()
        return carry

    def tile_arrival(hop, carry):
        source = lax.rem(index + n_same - hop, n_same)
        pltpu.make_async_remote_copy(
            src_ref=own_tile,
            dst_ref=tiles_ref.at[lax.div(source, n_blk), core, lax.rem(source, n_blk)],
            send_sem=tile_send.at[hop],
            recv_sem=tile_recv.at[source],
            device_id=(lax.div(source, n_blk) * 2 + core, lax.rem(source, n_blk)),
            device_id_type=MESH,
        ).wait_recv()
        return carry

    def over_copy(source, from_own):
        slot = tiles_ref.at[lax.div(source, n_blk), core, lax.rem(source, n_blk)]
        return pltpu.make_async_remote_copy(
            src_ref=own_tile if from_own else slot,
            dst_ref=slot,
            send_sem=over_send.at[source],
            recv_sem=over_recv.at[source],
            device_id=(z * 2 + 1 - core, blk),
            device_id_type=MESH,
        )

    def tile_over(hop, carry):
        tile_arrival(hop, carry)
        over_copy(lax.rem(index + n_same - hop, n_same), False).start()
        return carry

    def over_arrival(source, carry):
        slot = tiles_ref.at[lax.div(source, n_blk), 1 - core, lax.rem(source, n_blk)]
        pltpu.make_async_remote_copy(
            src_ref=slot,
            dst_ref=slot,
            send_sem=over_send.at[source],
            recv_sem=over_recv.at[source],
            device_id=(z * 2 + 1 - core, blk),
            device_id_type=MESH,
        ).wait_recv()
        return carry

    lax.fori_loop(1, n_same, tile_start, 0)
    over_copy(index, True).start()

    for part in range(2):
        pl.when(z > 0)(lambda: go_left(None, part).wait_send())
        pl.when(z < chain - 1)(lambda: go_right(None, part).wait_send())
        go_over(None, part).wait_send()

        def settle(origin, side):
            if side == "left":
                pl.when(z < chain - 1)(lambda: go_right(origin, part).wait_send())
            else:
                pl.when(z > 0)(lambda: go_left(origin, part).wait_send())
            go_over(origin, part).wait_send()

        for step in range(1, chain):
            each_of_step(step, settle)

    def settle_kv(origin, carry):
        for part in range(2):
            for hop in range(1, n_blk):
                kv_copy(origin, part, hop).wait_send()
        return carry

    lax.fori_loop(0, chain, settle_kv, 0)
    for copy in keeps:
        copy.wait()

    def settle_vel(hop, carry):
        other = lax.rem(seq + hop, n_seq)
        vel_copy(lax.div(other, 2), lax.rem(other, 2)).wait_send()
        return carry

    lax.fori_loop(1, n_seq, settle_vel, 0)

    keep.wait()
    lax.fori_loop(1, n_same, tile_over, 0)

    def settle_tile(hop, carry):
        tile_copy(hop).wait_send()
        over_copy(lax.rem(index + n_same - hop, n_same), False).wait_send()
        return carry

    lax.fori_loop(1, n_same, settle_tile, 0)
    over_copy(index, True).wait_send()
    lax.fori_loop(0, n_same, over_arrival, 0)


def latent_tiles(
    n_seq, n_blk, tokens, project_weight, noisy_latent, final_weight, conv_weight, gain, shift
):
    chain = n_seq // 2
    rows, depth = tokens.shape
    width = project_weight.shape[2]
    channels = conv_weight.shape[1]
    heads = width // HEAD_DIM
    pair = 2 * rows
    dma = pltpu.SemaphoreType.DMA
    vmem = pl.BlockSpec(memory_space=pltpu.VMEM)
    hbm = pl.BlockSpec(memory_space=pl.ANY)
    kept = [
        ((channels, TAPS), BF16),
        ((channels, 2 * TAPS), BF16),
        ((channels, 128), F32),
        ((TILE_VOX, TILE_VOX), BF16),
    ]
    return pl.pallas_call(
        functools.partial(attention_kernel, chain, n_blk),
        out_shape=[jax.ShapeDtypeStruct((chain, 2, n_blk, LATENT_CH, TILE_VOX), BF16)]
        + [jax.ShapeDtypeStruct(*one) for one in kept],
        in_specs=[hbm, hbm] + [vmem] * 5,
        out_specs=[hbm] * 5,
        scratch_shapes=[
            pltpu.VMEM((chain, 2, 2, rows // 2, depth), BF16),
            pltpu.VMEM(project_weight.shape, BF16),
            pltpu.VMEM((chain, pair, width), BF16),
            pltpu.VMEM((chain, 2, 2, n_blk * rows, width), BF16),
            pltpu.VMEM((chain, heads, pair, 2 * HEAD_DIM), F32),
            pltpu.VMEM((chain, heads, pair, HEAD_DIM), F32),
            pltpu.VMEM((n_seq, noisy_latent.shape[0], rows), BF16),
            pltpu.VMEM((n_seq, noisy_latent.shape[0], rows), BF16),
            pltpu.VMEM((LATENT_CH, TILE_VOX), BF16),
            pltpu.VMEM((4, rows, TILE_VOX), BF16),
        ]
        + [pltpu.VMEM(*one) for one in kept]
        + [
            dma((3,)),
            dma((4,)),
            dma((chain, 2, 3)),
            dma((chain, 2, 2)),
            dma((chain, 2, n_blk)),
            dma((chain, 2, n_blk)),
            dma((n_seq,)),
            dma((n_seq,)),
            dma((chain * n_blk,)),
            dma((chain * n_blk,)),
            dma((chain * n_blk,)),
            dma((chain * n_blk,)),
        ],
        compiler_params=pltpu.CompilerParams(
            collective_id=0, has_side_effects=True, vmem_limit_bytes=60 * 2**20
        ),
        name="attention_to_tiles",
    )(tokens, project_weight, noisy_latent, final_weight, conv_weight, gain, shift)


def decode_kernel(
    n_blk,
    count_ref,
    inter_ref,
    tiles_ref,
    weight_first,
    weight_second,
    affine,
    place,
    out_ref,
    patches,
    upper_early,
    upper_late,
    lower_early,
    lower_late,
):
    slot = pl.program_id(0)
    rank = lax.axis_index("seq") * n_blk + lax.axis_index("blk")
    channels = weight_first.shape[0]
    some_ch = channels // 2
    group = channels // GROUPS
    half_vox = TILE_VOX // TILE_F
    inv = 1.0 / (group * TILE_F * FRAME)

    def gather():
        first = lax.fori_loop(0, rank, lambda i, total: total + count_ref[i], 0)
        stack = []
        for number in range(MAXPIX):
            pixel = jnp.minimum(first + number, inter_ref.shape[1] - 1)
            pieces = [tiles_ref[inter_ref[k, pixel]] for k in range(4)]
            for side in range(2):
                for frame in range(TILE_F):
                    lanes = slice(frame * half_vox, (frame + 1) * half_vox)
                    stack.append(
                        jnp.concatenate(
                            [pieces[2 * side][:, lanes], pieces[2 * side + 1][:, lanes]], axis=1
                        )
                    )
        strips = jnp.dot(jnp.concatenate(stack, axis=0), place[...], preferred_element_type=F32)
        held = TILE_F * LATENT_CH
        for number in range(MAXPIX):
            base = number * 2 * held
            region = jnp.concatenate(
                [strips[base : base + held], strips[base + held : base + 2 * held]], axis=1
            )
            lane = lax.broadcasted_iota(jnp.int32, region.shape, 1)
            column = lane & (REGION_COLS - 1)
            row = lane >> 5
            by_row = [
                jnp.where(row == 0, region, pltpu.roll(region, REGION_COLS, 1)),
                region,
                jnp.where(
                    row == REGION_ROWS - 1, region, pltpu.roll(region, FRAME - REGION_COLS, 1)
                ),
            ]
            for b in range(3):
                moved = by_row[b]
                by_col = [
                    jnp.where(column == 0, moved, pltpu.roll(moved, 1, 1)),
                    moved,
                    jnp.where(column == REGION_COLS - 1, moved, pltpu.roll(moved, FRAME - 1, 1)),
                ]
                for g in range(3):
                    tap = by_col[g].astype(BF16)
                    for frame in range(TILE_F):
                        start = frame * TAPS + (b * 3 + g) * LATENT_CH
                        patches[number, pl.ds(start, LATENT_CH), :] = tap[
                            frame * LATENT_CH : (frame + 1) * LATENT_CH
                        ]

    def convolve(number, side, early, late):
        some = pl.ds(side * some_ch, some_ch)
        early[...] = jnp.dot(
            weight_first[some, :], patches[number, :TAPS, :], preferred_element_type=F32
        )
        late[...] = jnp.dot(weight_second[some, :], patches[number], preferred_element_type=F32)

    def finish(side, early, late):
        parts = [x[...].reshape(some_ch // group, group, FRAME) for x in (early, late)]
        mean = jnp.sum(parts[0] + parts[1], axis=(1, 2), keepdims=True) * inv
        spread = jnp.square(parts[0] - mean) + jnp.square(parts[1] - mean)
        var = jnp.sum(spread, axis=(1, 2), keepdims=True) * inv
        both = affine[pl.ds(side * some_ch, some_ch), :]
        gain = both[:, 0:1].reshape(some_ch // group, group, 1)
        shift = both[:, 1:2].reshape(some_ch // group, group, 1)
        slope = 0.5 * gain * lax.rsqrt(var + norm_eps)
        offset = 0.5 * shift - mean * slope
        filled = slot < count_ref[rank]
        slope = jnp.where(filled, slope, 0.0)
        offset = jnp.where(filled, offset, 0.0)
        for frame in range(TILE_F):
            half = parts[frame] * slope + offset
            value = half + half * jnp.tanh(half)
            out_ref[0, 0, pl.ds(side * some_ch, some_ch), pl.ds(frame * FRAME, FRAME)] = (
                value.reshape(some_ch, FRAME).astype(BF16)
            )

    @pl.when(slot == 0)
    def begin():
        gather()
        convolve(0, 0, upper_early, upper_late)

    convolve(slot, 1, lower_early, lower_late)
    finish(0, upper_early, upper_late)
    convolve(jnp.minimum(slot + 1, MAXPIX - 1), 0, upper_early, upper_late)
    finish(1, lower_early, lower_late)


def decode(n_blk, tiles, prepared, owner_count, intersection):
    channels = prepared[0].shape[0]
    voxels = TILE_F * FRAME
    whole = lambda x: pl.BlockSpec(x.shape, lambda i, *_: (0,) * x.ndim)
    return pl.pallas_call(
        functools.partial(decode_kernel, n_blk),
        out_shape=jax.ShapeDtypeStruct((1, MAXPIX, channels, voxels), BF16),
        grid_spec=pltpu.PrefetchScalarGridSpec(
            num_scalar_prefetch=2,
            grid=(MAXPIX,),
            in_specs=[whole(tiles)] + [whole(x) for x in prepared],
            out_specs=pl.BlockSpec((1, 1, channels, voxels), lambda i, *_: (0, i, 0, 0)),
            scratch_shapes=[pltpu.VMEM((MAXPIX, 2 * TAPS, FRAME), BF16)]
            + [pltpu.VMEM((channels // 2, FRAME), F32)] * 4,
        ),
        compiler_params=pltpu.CompilerParams(vmem_limit_bytes=60 * 2**20),
        name="decode_tiles",
    )(owner_count, intersection.T, tiles, *prepared)


def body(
    n_seq,
    n_blk,
    tokens,
    project_weight,
    noisy_latent,
    final_weight,
    conv_weight,
    norm_gain,
    norm_shift,
    owner_count,
    intersection,
):
    tiles, *prepared = latent_tiles(
        n_seq,
        n_blk,
        tokens,
        project_weight,
        noisy_latent.T,
        final_weight.T,
        conv_weight,
        norm_gain.reshape(1, -1),
        norm_shift.reshape(1, -1),
    )
    tiles = tiles.reshape(-1, LATENT_CH, TILE_VOX)
    return decode(n_blk, tiles, prepared, owner_count, intersection)


def solution(mesh):
    return jax.shard_map(
        functools.partial(body, mesh.shape["seq"], mesh.shape["blk"]),
        mesh=mesh,
        in_specs=(
            P(("seq", "blk"), None),
            P(None, None, "seq"),
            P(("seq", "blk"), None),
            P(),
            P(),
            P(),
            P(),
            P(),
            P(),
        ),
        out_specs=P(("seq", "blk"), None, None, None),
        check_vma=False,
    )
```

profile of v0, /device:TPU:0, one launch (start us, length us, event | category | flops | bytes accessed | tf_op | source)
XLA Modules:
  0.0 101.3 jit_solution(17903721818467068949)
XLA Ops:
  0.0 87.8 %attention_to_tiles.1 = (bf16[4,2,4,16,512]{4,3,2,1,0:T(8,128)(2,1)}, bf16[512,144]{1,0:T(8,128)(2,1)}, bf16[512,288]{1,0:T(8,128)(2,1)}, f32[512,128]{1,0:T(8,128)}, bf16[512,512]{1,0:T(8,128)(2,1)}) custom-call(bf16[128,3072]{1,0:T(8,128)(2,1)} %tokens_ref.1, bf16[3,3072,256]{2,1,0:T(8,128)(2,1)} %weight_ref.1, f32[64,128]{1,0:T(8,128)} %bitcast.8, ...), custom_call_target="tpu_custom_call" | custom-call | tf_op jit(solution)/shard_map/attention_to_tiles/pallas_call | solution.py:497
  87.8 13.5 %decode_tiles.1 = bf16[1,4,512,2048]{3,2,1,0:T(8,128)(2,1)} custom-call(s32[32]{0:T(128)} %count_ref.1, s32[4,64]{1,0:T(4,128)} %bitcast.11, bf16[32,16,512]{2,1,0:T(8,128)(2,1)} %bitcast.6, bf16[512,144]{1,0:T(8,128)(2,1)} %get-tuple-element.11.weight_first, bf16[512,288]{1,0:T(8,128)(2,1)} %get-tuple-element.12.weight_second, ...), custom_call_target="tpu_custom_call" | custom-call | tf_op jit(solution)/shard_map/decode_tiles/pallas_call | solution.py:649
where the time goes:
time: 102 us; the launch traced here: 101 us
  Pallas kernels  101 us (99%)
    pallas_call x1, Pallas kernels, latent_tiles(): pl.pallas_call(functools.partial(attention_kernel, chain, n_blk), out_sha...  87.8 us
    pallas_call x1, Pallas kernels, decode(): pl.pallas_call(functools.partial(decode_kernel, n_blk), out_shape=jax.Sha...  13.5 us

commit v1 on v0

--- a/solution.py
+++ b/solution.py
@@ -102,18 +102,18 @@
 
     barrier = pltpu.get_barrier_semaphore()
 
-    def greet(step, carry):
-        other = lax.rem(me + step, n_seq * n_blk)
+    def greet(target_seq, target_blk):
         pl.semaphore_signal(
-            barrier,
-            inc=1,
-            device_id=(lax.div(other, n_blk), lax.rem(other, n_blk)),
-            device_id_type=MESH,
-        )
-        return carry
-
-    lax.fori_loop(1, n_seq * n_blk, greet, 0)
-    pl.semaphore_wait(barrier, n_seq * n_blk - 1)
+            barrier, inc=1, device_id=(target_seq, target_blk), device_id_type=MESH
+        )
+
+    greet(seq + 1 - 2 * core, blk)
+    pl.when(z > 0)(lambda: greet(seq - 2, blk))
+    pl.when(z < chain - 1)(lambda: greet(seq + 2, blk))
+    for hop in range(1, n_blk):
+        greet(seq, lax.rem(blk + hop, n_blk))
+    ends = jnp.where(z > 0, 1, 0) + jnp.where(z < chain - 1, 1, 0)
+    pl.semaphore_wait(barrier, n_blk + ends)
 
     def tok_copy(origin, part, side, target_z, target_core):
         if origin is None:
@@ -190,20 +190,32 @@
             acc_all[origin, head, some, :] = jnp.zeros((rows, 2 * HEAD_DIM), F32)
 
     def attend(q_pair, kv_pair, part):
-        for head in range(heads):
-            lanes = pl.ds(head * HEAD_DIM, HEAD_DIM)
-            scores = nt_dot(q_all[q_pair, :, lanes], kv_all[kv_pair, part, 0, :, lanes])
-            old_max = max_all[q_pair, head]
-            new_max = jnp.maximum(old_max, jnp.max(scores, axis=1, keepdims=True))
-            rescale = jnp.exp2(old_max - new_max)
-            weights = jnp.exp2(scores - new_max[:, :1]).astype(BF16)
-            value = kv_all[kv_pair, part, 1, :, lanes]
-            value = jnp.concatenate([value, jnp.ones_like(value)], axis=1)
-            product = jnp.dot(weights, value, preferred_element_type=F32)
-            acc_all[q_pair, head] = (
-                acc_all[q_pair, head] * jnp.concatenate([rescale, rescale], axis=1) + product
+        every = range(heads)
+        lanes = [pl.ds(head * HEAD_DIM, HEAD_DIM) for head in every]
+        scores = [
+            nt_dot(q_all[q_pair, :, lanes[h]], kv_all[kv_pair, part, 0, :, lanes[h]])
+            for h in every
+        ]
+        values = [kv_all[kv_pair, part, 1, :, lanes[h]] for h in every]
+        old_max = [max_all[q_pair, h] for h in every]
+        old_acc = [acc_all[q_pair, h] for h in every]
+        new_max = [
+            jnp.maximum(old_max[h], jnp.max(scores[h], axis=1, keepdims=True)) for h in every
+        ]
+        rescale = [jnp.exp2(old_max[h] - new_max[h]) for h in every]
+        weights = [jnp.exp2(scores[h] - new_max[h][:, :1]).astype(BF16) for h in every]
+        product = [
+            jnp.dot(
+                weights[h],
+                jnp.concatenate([values[h], jnp.ones_like(values[h])], axis=1),
+                preferred_element_type=F32,
             )
-            max_all[q_pair, head] = new_max
+            for h in every
+        ]
+        for h in every:
+            wide = jnp.concatenate([rescale[h], rescale[h]], axis=1)
+            acc_all[q_pair, h] = old_acc[h] * wide + product[h]
+            max_all[q_pair, h] = new_max[h]
 
     def each_of_step(step, action):
         if step >= chain:
@@ -301,7 +313,8 @@
         def meet(origin, side):
             for hop in range(1, n_blk):
                 kv_arrival(origin, part, hop)
-            over_known(step, lambda other: attend(other, origin, part))
+            if turn < 2 * chain - 1:
+                over_known(step, lambda other: attend(other, origin, part))
 
         each_of_step(step, meet)
 
@@ -320,6 +333,7 @@
 
     for turn in range(chain):
         q_pair = lax.rem(z + 1 + turn, chain)
+        pl.when((z == 0) | (z == chain - 1))(lambda: attend(q_pair, chain - 1 - z, 1))
         attended = []
         for head in range(heads):
             total = acc_all[q_pair, head]

time: 102 us -> 98 us (0.961)
  Pallas kernels: 101 us -> 97.8 us
    pallas_call x1, Pallas kernels: 87.8 us -> 84.3 us  [latent_tiles(): pl.pallas_call(functools.partial(attention_kernel, chain, n_blk), out_sha...]
where the time goes in v1:
time: 98 us; the launch traced here: 97.8 us
  Pallas kernels  97.8 us (100%)
    pallas_call x1, Pallas kernels, latent_tiles(): pl.pallas_call(functools.partial(attention_kernel, chain, n_blk), out_sha...  84.3 us
    pallas_call x1, Pallas kernels, decode(): pl.pallas_call(functools.partial(decode_kernel, n_blk), out_shape=jax.Sha...  13.5 us

profile of v1, /device:TPU:0, one launch (start us, length us, event | category | flops | bytes accessed | tf_op | source)
XLA Modules:
  0.0 97.8 jit_solution(12939237819726804817)
XLA Ops:
  0.0 84.3 %attention_to_tiles.1 = (bf16[4,2,4,16,512]{4,3,2,1,0:T(8,128)(2,1)}, bf16[512,144]{1,0:T(8,128)(2,1)}, bf16[512,288]{1,0:T(8,128)(2,1)}, f32[512,128]{1,0:T(8,128)}, bf16[512,512]{1,0:T(8,128)(2,1)}) custom-call(bf16[128,3072]{1,0:T(8,128)(2,1)} %tokens_ref.1, bf16[3,3072,256]{2,1,0:T(8,128)(2,1)} %weight_ref.1, f32[64,128]{1,0:T(8,128)} %bitcast.8, ...), custom_call_target="tpu_custom_call" | custom-call | tf_op jit(solution)/shard_map/attention_to_tiles/pallas_call | solution.py:511
  84.3 13.5 %decode_tiles.1 = bf16[1,4,512,2048]{3,2,1,0:T(8,128)(2,1)} custom-call(s32[32]{0:T(128)} %count_ref.1, s32[4,64]{1,0:T(4,128)} %bitcast.11, bf16[32,16,512]{2,1,0:T(8,128)(2,1)} %bitcast.6, bf16[512,144]{1,0:T(8,128)(2,1)} %get-tuple-element.11.weight_first, bf16[512,288]{1,0:T(8,128)(2,1)} %get-tuple-element.12.weight_second, ...), custom_call_target="tpu_custom_call" | custom-call | tf_op jit(solution)/shard_map/decode_tiles/pallas_call | solution.py:663

commit v2 on v1

--- a/solution.py
+++ b/solution.py
@@ -189,14 +189,16 @@
             max_all[origin, head, some, :] = jnp.full((rows, HEAD_DIM), -1e30, F32)
             acc_all[origin, head, some, :] = jnp.zeros((rows, 2 * HEAD_DIM), F32)
 
-    def attend(q_pair, kv_pair, part):
+    def attend(q_pair, kv_pair, *parts):
         every = range(heads)
+
+        def rows_of(kind, lane):
+            pieces = [kv_all[kv_pair, part, kind, :, lane] for part in parts]
+            return pieces[0] if len(pieces) == 1 else jnp.concatenate(pieces, axis=0)
+
         lanes = [pl.ds(head * HEAD_DIM, HEAD_DIM) for head in every]
-        scores = [
-            nt_dot(q_all[q_pair, :, lanes[h]], kv_all[kv_pair, part, 0, :, lanes[h]])
-            for h in every
-        ]
-        values = [kv_all[kv_pair, part, 1, :, lanes[h]] for h in every]
+        scores = [nt_dot(q_all[q_pair, :, lanes[h]], rows_of(0, lanes[h])) for h in every]
+        values = [rows_of(1, lanes[h]) for h in every]
         old_max = [max_all[q_pair, h] for h in every]
         old_acc = [acc_all[q_pair, h] for h in every]
         new_max = [
@@ -295,8 +297,7 @@
         project_arrived(part)(z, None)
 
     def attend_both(q_pair, kv_pair):
-        attend(q_pair, kv_pair, 0)
-        attend(q_pair, kv_pair, 1)
+        attend(q_pair, kv_pair, 0, 1)
 
     for turn in range(2 * chain):
         step, part = turn // 2, turn % 2

time: 98 us -> 97.1 us (level)
  no operation moved by 1% of the time
where the time goes in v2:
time: 97.1 us; the launch traced here: 97 us
  Pallas kernels  96.9 us (100%)
    pallas_call x1, Pallas kernels, latent_tiles(): pl.pallas_call(functools.partial(attention_kernel, chain, n_blk), out_sha...  83.5 us
    pallas_call x1, Pallas kernels, decode(): pl.pallas_call(functools.partial(decode_kernel, n_blk), out_shape=jax.Sha...  13.4 us

profile of v2, /device:TPU:0, one launch (start us, length us, event | category | flops | bytes accessed | tf_op | source)
XLA Modules:
  0.0 97.0 jit_solution(6693846788168667352)
XLA Ops:
  0.0 83.5 %attention_to_tiles.1 = (bf16[4,2,4,16,512]{4,3,2,1,0:T(8,128)(2,1)}, bf16[512,144]{1,0:T(8,128)(2,1)}, bf16[512,288]{1,0:T(8,128)(2,1)}, f32[512,128]{1,0:T(8,128)}, bf16[512,512]{1,0:T(8,128)(2,1)}) custom-call(bf16[128,3072]{1,0:T(8,128)(2,1)} %tokens_ref.1, bf16[3,3072,256]{2,1,0:T(8,128)(2,1)} %weight_ref.1, f32[64,128]{1,0:T(8,128)} %bitcast.8, ...), custom_call_target="tpu_custom_call" | custom-call | tf_op jit(solution)/shard_map/attention_to_tiles/pallas_call | solution.py:512
  83.5 13.4 %decode_tiles.1 = bf16[1,4,512,2048]{3,2,1,0:T(8,128)(2,1)} custom-call(s32[32]{0:T(128)} %count_ref.1, s32[4,64]{1,0:T(4,128)} %bitcast.11, bf16[32,16,512]{2,1,0:T(8,128)(2,1)} %bitcast.6, bf16[512,144]{1,0:T(8,128)(2,1)} %get-tuple-element.11.weight_first, bf16[512,288]{1,0:T(8,128)(2,1)} %get-tuple-element.12.weight_second, ...), custom_call_target="tpu_custom_call" | custom-call | tf_op jit(solution)/shard_map/decode_tiles/pallas_call | solution.py:664
